TPU v7x, 32 devices: a whole 2x2x4 slice. The times are simulated.
32 devices in a mesh: mem: 4 (over x, core), tile: 8 (over z, y).
Axes of the slice: x: 2, y: 2, z: 4, core: 2. Of those that a mesh axis runs over, the one named last changes fastest.
Arguments:
- control: float32 [8, 32, 320, 160], P('mem', None, 'tile'), may hold values from -6 to 6
- ens_perts: float32 [8, 2, 32, 320, 160], P('mem', None, None, 'tile'), may hold values from -8 to 8
- vert_corr: float32 [32, 32], replicated, may hold values from -1 to 1
- slab_wts: float32 [8, 4], replicated, may hold values from 0.25 to 2
- level_slab: int32 [32], replicated, may hold values from 0 to 7, as said below
Outputs:
- wind_share: float32 [2, 32, 320, 160], P(None, 'mem', 'tile')
- gradient: float32 [8, 32, 320, 160], P('mem', None, 'tile')
Inputs may be any that keep to these rules, and one draw needn't show every extreme that they name: `level_slab`: each slab holds a contiguous run of levels and slab numbers never fall with the level; every slab holds 1 to 8 levels, and one slab holds exactly 8.
All inputs are finite; a program needn't handle non-finite values.
Results may differ from a plain program's by a relative error of at most 0.0001.
Values sent between devices are 32-bit elements; how exact they have to be, the bound alone decides.
A program may use at most 128 MiB of HBM per device.

v0:
```python
import functools
import math

import jax
import jax.numpy as jnp
import ml_dtypes
import numpy as np
from jax import lax
from jax.experimental import pallas as pl
from jax.experimental.pallas import tpu as pltpu
from jax.sharding import PartitionSpec as P

dilation_steps = (1, 2, 4, 8)
highest = lax.Precision.HIGHEST
MESH = pl.DeviceIdType.MESH
bf16 = jnp.bfloat16
f32 = jnp.float32
LANES = 128
SUB = 8


def line_filter(length, dilation):
    positions = np.arange(length)
    distance = np.abs(positions[None, :] - positions[:, None])
    inside = (distance % dilation == 0) & (distance <= 6 * dilation)
    ratio = (distance // dilation).astype(np.float64)
    kernel = np.where(inside, np.exp(-ratio * ratio / 8.0), 0.0)
    cubed = kernel @ kernel @ kernel
    centre = cubed[:, length // 2]
    return cubed / np.sqrt(np.sum(centre * centre))


def two_parts(matrix):
    high = matrix.astype(ml_dtypes.bfloat16)
    low = (matrix - high.astype(np.float64)).astype(ml_dtypes.bfloat16)
    return high, low


def x_matrices(tiles, rows, rows_pad):
    place = (np.arange(tiles)[:, None] * rows_pad + np.arange(rows)[None, :]).reshape(-1)
    found = []
    for dilation in dilation_steps:
        full = np.zeros((tiles * rows_pad,) * 2)
        full[np.ix_(place, place)] = line_filter(tiles * rows, dilation)
        high, low = two_parts(full)
        found.append(np.concatenate([high, high, low], axis=1))
    return np.stack(found)


def y_matrices(cols, slots, rest):
    result = []
    for slot in range(slots):
        place = np.concatenate([np.arange(LANES), LANES + slot * rest + np.arange(rest)])
        stacked = []
        for dilation in dilation_steps:
            full = np.zeros((2 * LANES, 2 * LANES))
            full[np.ix_(place, place)] = line_filter(cols, dilation).T
            stacked.append(full)
        result.append(np.stack(two_parts(np.concatenate(stacked, axis=0))))
    return np.stack(result)


def selectors(levels, tiles, slots):
    one = np.eye(levels, dtype=np.float32)
    main = np.repeat(one, SUB, axis=0)
    tile_num = np.arange(tiles)
    outer = np.stack([np.repeat(one[slots * tile_num + j], SUB, axis=0) for j in range(slots)])
    inner = np.stack([
        np.concatenate([
            np.repeat(one[slots * tile_num + (j - r) % slots], SUB, axis=0) for r in range(slots)
        ])
        for j in range(slots)
    ])
    return main, outer, inner


def kernel(
    dims,
    control_ref, pert_hbm, vert_ref, wl_ref, gx_hbm, by_hbm, main_sel, outer_sel, inner_sel,
    wind_ref, grad_ref,
    pert_raw, gx, by, send_a, f_a, y_a, s_a, pert, wp, cr, ws, xr, wf, send_b, f_b, y_b,
    fs, xh, xl, mix_main, mix_rest, back_main, back_rest,
    load_sem, a1s, a1r, a2s, a2r, a3s, a3r, a4s, a4r, c1s, c1r, xs, xrs, c2s, c2r,
):
    nt, nm, members, comps, levels, rows, rows_pad, cols, slots, rest, scale, order = dims
    planes = slots + 1
    scales = len(dilation_steps)
    all_x = nt * rows_pad
    nx = nm // 2
    nh = nt // 2
    chunks = rows_pad // SUB
    s_b = f_a
    me = lax.axis_index("tile")
    mem = lax.axis_index("mem")
    chip, core = mem // 2, lax.rem(mem, 2)
    partner = chip * 2 + (1 - core)

    loads = [
        pltpu.make_async_copy(pert_hbm.at[0], pert_raw, load_sem.at[0]),
        pltpu.make_async_copy(gx_hbm, gx, load_sem.at[1]),
        pltpu.make_async_copy(by_hbm, by, load_sem.at[2]),
    ]
    for load in loads:
        load.start()

    def packed(block):
        parts = [block[i, :, LANES:cols] for i in range(slots)]
        if rest * slots < LANES:
            parts.append(jnp.zeros((rows, LANES - rest * slots), f32))
        return jnp.concatenate(parts, axis=-1)

    def pack_to(block, out):
        if rows_pad != rows:
            out[...] = jnp.zeros((planes, rows_pad, LANES), f32)
        out[0:slots, 0:rows, :] = block[:, :, 0:LANES]
        out[slots, 0:rows, :] = packed(block)

    def tile_rank(k):
        return lax.rem(me + k, nt)

    barrier = pltpu.get_barrier_semaphore()
    for k in range(1, nt):
        pl.semaphore_signal(barrier, inc=1, device_id={"tile": tile_rank(k)}, device_id_type=MESH)
    pl.semaphore_signal(barrier, inc=1, device_id={"mem": partner}, device_id_type=MESH)
    for k in range(1, nx):
        other = lax.rem(chip + k, nx) * 2 + core
        pl.semaphore_signal(barrier, inc=1, device_id={"mem": other}, device_id_type=MESH)

    def pack_control(m):
        def body(t, carry):
            pack_to(control_ref[m, pl.ds(slots * t, slots)], send_a.at[m, t])
            return carry
        lax.fori_loop(0, nt, body, 0)

    pack_control(0)
    pl.semaphore_wait(barrier, (nt - 1) + 1 + (nx - 1))

    def exchange(src, dst, m, row, size, send_sem, recv_sem):
        span = pl.ds(row, size)
        for k in order:
            d = tile_rank(k)
            pltpu.make_async_remote_copy(
                src_ref=src.at[m, d, :, span, :], dst_ref=dst.at[m, me, :, span, :],
                send_sem=send_sem, recv_sem=recv_sem, device_id={"tile": d}, device_id_type=MESH,
            ).start()
        pltpu.make_async_copy(
            src.at[m, me, :, span, :], dst.at[m, me, :, span, :], recv_sem
        ).start()

    def arrived(dst, m, row, size, recv_sem):
        there = dst.at[m, :, :, pl.ds(row, size), :]
        pltpu.make_async_copy(there, there, recv_sem).wait()

    def sent(src, m, row, size, send_sem):
        there = src.at[m, pl.ds(0, nt - 1), :, pl.ds(row, size), :]
        pltpu.make_async_copy(there, there, send_sem).wait()

    exchange(send_a, f_a, 0, 0, rows_pad, a1s.at[0], a1r.at[0])
    for m in range(1, members):
        pack_control(m)
        exchange(send_a, f_a, m, 0, rows_pad, a1s.at[m], a1r.at[m])

    vert = vert_ref[...]
    same_row = lambda a, b: (
        lax.rem(lax.broadcasted_iota(jnp.int32, (a, b), 0), SUB)
        == lax.rem(lax.broadcasted_iota(jnp.int32, (a, b), 1), SUB)
    )

    def spread(left, right, flip):
        dot = functools.partial(lax.dot_general, precision=highest, preferred_element_type=f32)
        first = dot(left, vert, (((1,), (1 if flip else 0,)), ((), ())))
        wide = dot(first, right, (((1,), (1,)), ((), ())))
        return jnp.where(same_row(*wide.shape), wide, 0.0)

    for flip, main_out, rest_out in ((False, mix_main, mix_rest), (True, back_main, back_rest)):
        main_out[...] = spread(main_sel[...], main_sel[...], flip)
        for j in range(slots):
            rest_out[pl.ds(j * nt * SUB, nt * SUB), :] = spread(outer_sel[j], inner_sel[j], flip)

    for m in range(members):
        load = pltpu.make_async_copy(pert_hbm.at[m], pert_raw, load_sem.at[0])
        if m > 0:
            load.start()
        load.wait()

        def pack_pert(n, carry):
            c, t = n // nt, lax.rem(n, nt)
            pack_to(pert_raw[c, pl.ds(slots * t, slots)], pert.at[m, c, t])
            return carry
        lax.fori_loop(0, comps * nt, pack_pert, 0)
    loads[1].wait()
    loads[2].wait()

    def smooth(src, m, out):
        wide = jnp.concatenate(
            [src[m, :, p].reshape(all_x, LANES) for p in range(planes)], axis=1
        )
        high = wide.astype(bf16)
        low = (wide - high.astype(f32)).astype(bf16)
        fs[0:all_x, :] = high
        fs[all_x:2 * all_x, :] = low
        fs[2 * all_x:3 * all_x, :] = high

        def along_x(s, carry):
            stepped = jnp.dot(gx[s], fs[...], preferred_element_type=f32) * wl_ref[pl.ds(s, 1), :]
            up = stepped.astype(bf16)
            down = (stepped - up.astype(f32)).astype(bf16)
            for p in range(planes):
                xh[s, p] = up[:, p * LANES:(p + 1) * LANES]
                xl[s, p] = down[:, p * LANES:(p + 1) * LANES]
            return carry
        lax.fori_loop(0, scales, along_x, 0)

        def along_y(i, carry):
            pick = lambda ref: jnp.concatenate(
                [ref[s, p] for s in range(scales) for p in (i, slots)], axis=1
            )
            up, down = pick(xh), pick(xl)
            got = jnp.dot(up, by[i, 0], preferred_element_type=f32)
            got = got + jnp.dot(down, by[i, 0], preferred_element_type=f32)
            got = got + jnp.dot(up, by[i, 1], preferred_element_type=f32)
            got = got.reshape(nt, rows_pad, 2 * LANES)
            out[m, :, i] = got[:, :, 0:LANES]
            return carry + got[:, :, LANES:]
        rest_sum = lax.fori_loop(0, slots, along_y, jnp.zeros((nt, rows_pad, LANES), f32))
        out[m, :, slots] = rest_sum

    lane_group = lax.broadcasted_iota(jnp.int32, (nt * SUB, members * LANES), 1) % LANES // rest

    def mix(main_in, rest_in, main_mat, rest_mat):
        main_out = jnp.dot(main_mat[...], jnp.concatenate(main_in, axis=1),
                           precision=highest, preferred_element_type=f32)
        rolled = jnp.concatenate([
            jnp.concatenate(
                [x if r == 0 else pltpu.roll(x, r * rest, 1) for r in range(slots)], axis=0)
            for x in rest_in
        ], axis=1)
        rest_all = jnp.dot(rest_mat[...], rolled, precision=highest, preferred_element_type=f32)
        rest_out = jnp.zeros((nt * SUB, members * LANES), f32)
        for j in range(slots):
            rest_out = jnp.where(
                lane_group == j, rest_all[j * nt * SUB:(j + 1) * nt * SUB], rest_out)
        mains = [main_out[:, m * LANES:(m + 1) * LANES].reshape(nt, slots, SUB, LANES)
                 for m in range(members)]
        rests = [rest_out[:, m * LANES:(m + 1) * LANES].reshape(nt, SUB, LANES)
                 for m in range(members)]
        return mains, rests

    def span_of(c):
        return pl.ds(c * SUB, SUB)

    def core_copy(c, which):
        span = span_of(c)
        if which == 1:
            src, dst = wp.at[:, pl.ds((1 - core) * nh, nh), :, span, :], cr.at[:, :, :, span, :]
            sems = c1s.at[c], c1r.at[c]
        else:
            own = wf.at[:, pl.ds(core * nh, nh), :, span, :]
            src, dst, sems = own, own, (c2s.at[c], c2r.at[c])
        return pltpu.make_async_remote_copy(
            src_ref=src, dst_ref=dst, send_sem=sems[0], recv_sem=sems[1],
            device_id={"mem": partner}, device_id_type=MESH)

    def chip_copy(c, k):
        span = span_of(c)
        other = lax.rem(chip + k, nx) * 2 + core
        return pltpu.make_async_remote_copy(
            src_ref=ws.at[:, :, :, span, :], dst_ref=xr.at[k - 1, :, :, :, span, :],
            send_sem=xs.at[c, k - 1], recv_sem=xrs.at[c, k - 1],
            device_id={"mem": other}, device_id_type=MESH)

    def stage_mix(c):
        span = span_of(c)
        for m in range(members):
            arrived(s_a, m, c * SUB, SUB, a2r.at[m, c])
        mains, rests = mix(
            [s_a[m, :, 0:slots, span, :].reshape(levels * SUB, LANES) for m in range(members)],
            [s_a[m, :, slots, span, :].reshape(nt * SUB, LANES) for m in range(members)],
            mix_main, mix_rest)
        for comp in range(comps):
            main = pert[0, comp, :, 0:slots, span, :] * mains[0]
            tail = pert[0, comp, :, slots, span, :] * rests[0]
            for m in range(1, members):
                main = main + pert[m, comp, :, 0:slots, span, :] * mains[m]
                tail = tail + pert[m, comp, :, slots, span, :] * rests[m]
            wp[comp, :, 0:slots, span, :] = main
            wp[comp, :, slots, span, :] = tail
        core_copy(c, 1).start()

    def stage_chip(c):
        span = span_of(c)
        core_copy(c, 1).wait_recv()
        ws[:, :, :, span, :] = wp[:, pl.ds(core * nh, nh), :, span, :] + cr[:, :, :, span, :]
        for k in range(1, nx):
            chip_copy(c, k).start()

    def stage_full(c):
        span = span_of(c)
        total = ws[:, :, :, span, :]
        for k in range(1, nx):
            chip_copy(c, k).wait_recv()
            total = total + xr[k - 1, :, :, :, span, :]
        wf[:, pl.ds(core * nh, nh), :, span, :] = total * scale
        core_copy(c, 2).start()

    def stage_back(c):
        span = span_of(c)
        other_half = wf.at[:, pl.ds((1 - core) * nh, nh), :, span, :]
        pltpu.make_async_copy(other_half, other_half, c2r.at[c]).wait()
        mains, rests = [], []
        for m in range(members):
            main = pert[m, 0, :, 0:slots, span, :] * wf[0, :, 0:slots, span, :]
            tail = pert[m, 0, :, slots, span, :] * wf[0, :, slots, span, :]
            for comp in range(1, comps):
                main = main + pert[m, comp, :, 0:slots, span, :] * wf[comp, :, 0:slots, span, :]
                tail = tail + pert[m, comp, :, slots, span, :] * wf[comp, :, slots, span, :]
            mains.append((main * scale).reshape(levels * SUB, LANES))
            rests.append((tail * scale).reshape(nt * SUB, LANES))
        mains, rests = mix(mains, rests, back_main, back_rest)
        for m in range(members):
            send_b[m, :, 0:slots, span, :] = mains[m]
            send_b[m, :, slots, span, :] = rests[m]
            exchange(send_b, f_b, m, c * SUB, SUB, a3s.at[m, c], a3r.at[m, c])

    early = min(2, chunks)
    give_back = lambda m, c: exchange(y_a, s_a, m, c * SUB, SUB, a2s.at[m, c], a2r.at[m, c])
    for m in range(members):
        arrived(f_a, m, 0, rows_pad, a1r.at[m])
        smooth(f_a, m, y_a)
        for c in range(early):
            give_back(m, c)
    for c in range(early, chunks):
        for m in range(members):
            give_back(m, c)

    for step in range(chunks + 3):
        if 0 <= step - 3 < chunks:
            stage_back(step - 3)
        if 0 <= step - 2 < chunks:
            stage_full(step - 2)
        if 0 <= step - 1 < chunks:
            stage_chip(step - 1)
        if step < chunks:
            stage_mix(step)

    share = wind_ref.shape[1] // slots
    for comp in range(comps):
        for t in range(share):
            for i in range(slots):
                got = wf.at[comp, mem * share + t]
                wind_ref[comp, t * slots + i, :, 0:LANES] = got[i, 0:rows, :]
                wind_ref[comp, t * slots + i, :, LANES:cols] = got[slots, 0:rows, i * rest:(i + 1) * rest]

    for m in range(members):
        for c in range(chunks):
            arrived(f_b, m, c * SUB, SUB, a3r.at[m, c])
        smooth(f_b, m, y_b)
        exchange(y_b, s_b, m, 0, rows_pad, a4s.at[m], a4r.at[m])

    for m in range(members):
        arrived(s_b, m, 0, rows_pad, a4r.at[m])

        def finish(t, carry):
            for i in range(slots):
                lev = slots * t + i
                grad_ref[m, lev, :, 0:LANES] = (
                    control_ref[m, lev, :, 0:LANES] + s_b[m, t, i, 0:rows, :])
                grad_ref[m, lev, :, LANES:cols] = (
                    control_ref[m, lev, :, LANES:cols]
                    + s_b[m, t, slots, 0:rows, i * rest:(i + 1) * rest])
            return carry
        lax.fori_loop(0, nt, finish, 0)

    for m in range(members):
        sent(send_a, m, 0, rows_pad, a1s.at[m])
        sent(y_b, m, 0, rows_pad, a4s.at[m])
        for c in range(chunks):
            sent(y_a, m, c * SUB, SUB, a2s.at[m, c])
            sent(send_b, m, c * SUB, SUB, a3s.at[m, c])
    for c in range(chunks):
        core_copy(c, 1).wait_send()
        core_copy(c, 2).wait_send()
        for k in range(1, nx):
            chip_copy(c, k).wait_send()


def shards(mesh, control, ens_perts, vert_corr, slab_wts, level_slab):
    members, levels, rows, cols = control.shape
    comps = ens_perts.shape[1]
    nt, nm = mesh.shape["tile"], mesh.shape["mem"]
    slots = levels // nt
    planes = slots + 1
    rest = cols - LANES
    rows_pad = -(-rows // SUB) * SUB
    all_x = nt * rows_pad
    chunks = rows_pad // SUB
    nx, nh = nm // 2, nt // 2
    scale = 1.0 / math.sqrt(members * nm - 1)
    scales = len(dilation_steps)

    choose = (level_slab[:, None] == jnp.arange(slab_wts.shape[0])[None, :]).astype(f32)
    mine = lax.dynamic_slice_in_dim(choose, lax.axis_index("tile") * slots, slots, 0)
    mine = jnp.sum(mine[:, :, None] * slab_wts[None], axis=1)
    main_w = jnp.broadcast_to(mine.T[:, :, None], (scales, slots, LANES)).reshape(scales, -1)
    rest_w = jnp.broadcast_to(mine.T[:, :, None], (scales, slots, rest)).reshape(scales, -1)
    rest_w = jnp.pad(rest_w, ((0, 0), (0, LANES - rest * slots)))
    lane_wts = jnp.concatenate([main_w, rest_w], axis=1)

    gx = jnp.asarray(x_matrices(nt, rows, rows_pad))
    by = jnp.asarray(y_matrices(cols, slots, rest))
    picks = [jnp.asarray(a) for a in selectors(levels, nt, slots)]
    order = tuple(sorted(range(1, nt), key=lambda k: (abs(k - nt / 2), k)))
    dims = (nt, nm, members, comps, levels, rows, rows_pad, cols, slots, rest, scale, order)

    vmem = pl.BlockSpec(memory_space=pltpu.VMEM)
    anyspace = pl.BlockSpec(memory_space=pl.ANY)
    fields = pltpu.VMEM((members, nt, planes, rows_pad, LANES), f32)
    halfway = (comps, nh, planes, rows_pad, LANES)
    whole_wind = pltpu.VMEM((comps, nt, planes, rows_pad, LANES), f32)
    square = pltpu.VMEM((levels * SUB, levels * SUB), f32)
    dma = pltpu.SemaphoreType.DMA
    return pl.pallas_call(
        functools.partial(kernel, dims),
        out_shape=(
            jax.ShapeDtypeStruct((comps, levels // nm, rows, cols), f32),
            jax.ShapeDtypeStruct(control.shape, f32),
        ),
        in_specs=[vmem, anyspace, vmem, vmem, anyspace, anyspace, vmem, vmem, vmem],
        out_specs=(vmem, vmem),
        scratch_shapes=[
            pltpu.VMEM(ens_perts.shape[1:], f32),
            pltpu.VMEM(gx.shape, bf16),
            pltpu.VMEM(by.shape, bf16),
            fields, fields, fields, fields,
            pltpu.VMEM((members, comps, nt, planes, rows_pad, LANES), f32),
            whole_wind,
            pltpu.VMEM(halfway, f32),
            pltpu.VMEM(halfway, f32),
            pltpu.VMEM((nx - 1,) + halfway, f32),
            whole_wind,
            fields, fields, fields,
            pltpu.VMEM((3 * all_x, planes * LANES), bf16),
            pltpu.VMEM((scales, planes, all_x, LANES), bf16),
            pltpu.VMEM((scales, planes, all_x, LANES), bf16),
            square, square, square, square,
            dma((3,)),
            dma((members,)), dma((members,)),
            dma((members, chunks)), dma((members, chunks)),
            dma((members, chunks)), dma((members, chunks)),
            dma((members,)), dma((members,)),
            dma((chunks,)), dma((chunks,)),
            dma((chunks, nx - 1)), dma((chunks, nx - 1)),
            dma((chunks,)), dma((chunks,)),
        ],
        compiler_params=pltpu.CompilerParams(
            collective_id=0, has_side_effects=True, vmem_limit_bytes=58 * 2 ** 20),
        cost_estimate=pl.CostEstimate(
            flops=12 * 10 ** 9, bytes_accessed=30 * 10 ** 6, transcendentals=0),
    )(control, ens_perts, vert_corr, lane_wts, gx, by, *picks)


def solution(mesh):
    return jax.shard_map(
        functools.partial(shards, mesh),
        mesh=mesh,
        in_specs=(P("mem", None, "tile", None), P("mem", None, None, "tile", None), P(), P(), P()),
        out_specs=(P(None, "mem", "tile", None), P("mem", None, "tile", None)),
        check_vma=False,
    )
```

profile of v0, /device:TPU:13, one launch (start us, length us, event | category | flops | bytes accessed | tf_op | source)
XLA Modules:
  0.0 166.9 jit_solution(3103793868979097157)
XLA Ops:
  0.6 0.7 dynamic-slice
  1.4 0.1 fusion
  1.4 0.8 multiply_reduce_fusion
  2.2 0.1 copy.13
  2.3 0.1 broadcast_in_dim.5
  2.4 0.1 reshape.15
  2.5 0.1 broadcast_bitcast_fusion
  2.5 0.6 pad_maximum_fusion.wl_ref
  3.2 158.3 %shard_map.113 = (f32[2,8,40,160]{3,2,1,0:T(8,128)}, f32[2,32,40,160]{3,2,1,0:T(8,128)}) custom-call(f32[2,32,40,160]{3,2,1,0:T(8,128)} %control_ref.1, f32[2,2,32,40,160]{4,3,2,1,0:T(8,128)} %pert_hbm.1, f32[32,32]{1,0:T(8,128)} %vert_ref.1, f32[4,640]{1,0:T(4,128)} %pad_maximum_fusion.wl_ref, bf16[4,320,960]{2,1,0:T(8,128)(2,1)} %constant.22.clone.gx_hbm, ...), custom_call_target="tpu_custom_call" | custom-call | flops 12000000000 | bytes 30000000 | tf_op jit(solution)/shard_map/pallas_call | solution.py:422
  161.5 2.0 %copy.20 = f32[2,8,40,160]{3,2,1,0:T(8,128)} copy(f32[2,8,40,160]{3,2,1,0:T(8,128)} %get-tuple-element.4) | data formatting | bytes 819200
  163.5 3.4 %copy.21 = f32[2,32,40,160]{3,2,1,0:T(8,128)} copy(f32[2,32,40,160]{3,2,1,0:T(8,128)} %get-tuple-element.5) | data formatting | bytes 3276800
  (1 shorter events, 0.0 us)
where the time goes:
time: 167 us
  Pallas kernels  158 us (95%)
  local copies, waits for them, and re-layouts  6.47 us (4%)
    pallas_call x1, Pallas kernels, shards(): pl.pallas_call(functools.partial(kernel, dims), out_shape=(jax.ShapeDtype...  158 us
    unnamed x4, local copies, waits for them, and re-layouts  5.48 us

commit v1 on v0

--- a/solution.py
+++ b/solution.py
@@ -76,10 +76,10 @@
 
 def kernel(
     dims,
-    control_ref, pert_hbm, vert_ref, wl_ref, gx_hbm, by_hbm, main_sel, outer_sel, inner_sel,
-    wind_ref, grad_ref,
+    control_ref, pert_hbm, vert_ref, slab_ref, level_ref, gx_hbm, by_hbm, main_sel, outer_sel, inner_sel,
+    wind_ref, back_ref,
     pert_raw, gx, by, send_a, f_a, y_a, s_a, pert, wp, cr, ws, xr, wf, send_b, f_b, y_b,
-    fs, xh, xl, mix_main, mix_rest, back_main, back_rest,
+    fs, xh, xl, wl_ref, mix_main, mix_rest, back_main, back_rest,
     load_sem, a1s, a1r, a2s, a2r, a3s, a3r, a4s, a4r, c1s, c1r, xs, xrs, c2s, c2r,
 ):
     nt, nm, members, comps, levels, rows, rows_pad, cols, slots, rest, scale, order = dims
@@ -161,6 +161,15 @@
         exchange(send_a, f_a, m, 0, rows_pad, a1s.at[m], a1r.at[m])
 
     vert = vert_ref[...]
+    slabs = slab_ref.shape[0]
+    column = lambda a, b: lax.dot_general(
+        a, b, (((0,), (0,)), ((), ())), precision=highest, preferred_element_type=f32)
+    choose = (
+        lax.broadcasted_iota(jnp.int32, (slabs, levels), 0) == level_ref[...]).astype(f32)
+    lane = lax.broadcasted_iota(jnp.int32, (levels, planes * LANES), 1)
+    lane_slot = jnp.where(lane < slots * LANES, lane // LANES, (lane - slots * LANES) // rest)
+    own = (lax.broadcasted_iota(jnp.int32, lane.shape, 0) == me * slots + lane_slot).astype(f32)
+    wl_ref[...] = column(column(choose, slab_ref[...]), own)
     same_row = lambda a, b: (
         lax.rem(lax.broadcasted_iota(jnp.int32, (a, b), 0), SUB)
         == lax.rem(lax.broadcasted_iota(jnp.int32, (a, b), 1), SUB)
@@ -303,6 +312,10 @@
         wf[:, pl.ds(core * nh, nh), :, span, :] = total * scale
         core_copy(c, 2).start()
 
+    early = min(2, chunks)
+    send_adjoint = lambda m, c: exchange(
+        send_b, f_b, m, c * SUB, SUB, a3s.at[m, c], a3r.at[m, c])
+
     def stage_back(c):
         span = span_of(c)
         other_half = wf.at[:, pl.ds((1 - core) * nh, nh), :, span, :]
@@ -320,9 +333,9 @@
         for m in range(members):
             send_b[m, :, 0:slots, span, :] = mains[m]
             send_b[m, :, slots, span, :] = rests[m]
-            exchange(send_b, f_b, m, c * SUB, SUB, a3s.at[m, c], a3r.at[m, c])
-
-    early = min(2, chunks)
+            if m == 0 or c < early:
+                send_adjoint(m, c)
+
     give_back = lambda m, c: exchange(y_a, s_a, m, c * SUB, SUB, a2s.at[m, c], a2r.at[m, c])
     for m in range(members):
         arrived(f_a, m, 0, rows_pad, a1r.at[m])
@@ -343,13 +356,12 @@
         if step < chunks:
             stage_mix(step)
 
-    share = wind_ref.shape[1] // slots
-    for comp in range(comps):
-        for t in range(share):
-            for i in range(slots):
-                got = wf.at[comp, mem * share + t]
-                wind_ref[comp, t * slots + i, :, 0:LANES] = got[i, 0:rows, :]
-                wind_ref[comp, t * slots + i, :, LANES:cols] = got[slots, 0:rows, i * rest:(i + 1) * rest]
+    for m in range(1, members):
+        for c in range(early, chunks):
+            send_adjoint(m, c)
+
+    share = wind_ref.shape[1]
+    wind_ref[...] = wf[:, pl.ds(mem * share, share)]
 
     for m in range(members):
         for c in range(chunks):
@@ -359,17 +371,7 @@
 
     for m in range(members):
         arrived(s_b, m, 0, rows_pad, a4r.at[m])
-
-        def finish(t, carry):
-            for i in range(slots):
-                lev = slots * t + i
-                grad_ref[m, lev, :, 0:LANES] = (
-                    control_ref[m, lev, :, 0:LANES] + s_b[m, t, i, 0:rows, :])
-                grad_ref[m, lev, :, LANES:cols] = (
-                    control_ref[m, lev, :, LANES:cols]
-                    + s_b[m, t, slots, 0:rows, i * rest:(i + 1) * rest])
-            return carry
-        lax.fori_loop(0, nt, finish, 0)
+        back_ref[m] = s_b[m]
 
     for m in range(members):
         sent(send_a, m, 0, rows_pad, a1s.at[m])
@@ -382,6 +384,30 @@
         core_copy(c, 2).wait_send()
         for k in range(1, nx):
             chip_copy(c, k).wait_send()
+
+
+def unpack_kernel(rest, control_ref, back_ref, wind_packed, grad_ref, wind_ref):
+    rows, cols = control_ref.shape[-2:]
+    slots = back_ref.shape[2] - 1
+
+    def level(tiles, t, i):
+        return (tiles[0, t, i, 0:rows, :], tiles[0, t, slots, 0:rows, i * rest:(i + 1) * rest])
+
+    for t in range(back_ref.shape[1]):
+        for i in range(slots):
+            lev = slots * t + i
+            main, tail = level(back_ref, t, i)
+            grad_ref[0, lev, :, 0:LANES] = control_ref[0, lev, :, 0:LANES] + main
+            grad_ref[0, lev, :, LANES:cols] = control_ref[0, lev, :, LANES:cols] + tail
+
+    @pl.when(pl.program_id(0) == 0)
+    def _():
+        for comp in range(wind_packed.shape[0]):
+            for t in range(wind_packed.shape[1]):
+                for i in range(slots):
+                    main, tail = level(wind_packed.at[pl.ds(comp, 1)], t, i)
+                    wind_ref[comp, slots * t + i, :, 0:LANES] = main
+                    wind_ref[comp, slots * t + i, :, LANES:cols] = tail
 
 
 def shards(mesh, control, ens_perts, vert_corr, slab_wts, level_slab):
@@ -398,14 +424,6 @@
     scale = 1.0 / math.sqrt(members * nm - 1)
     scales = len(dilation_steps)
 
-    choose = (level_slab[:, None] == jnp.arange(slab_wts.shape[0])[None, :]).astype(f32)
-    mine = lax.dynamic_slice_in_dim(choose, lax.axis_index("tile") * slots, slots, 0)
-    mine = jnp.sum(mine[:, :, None] * slab_wts[None], axis=1)
-    main_w = jnp.broadcast_to(mine.T[:, :, None], (scales, slots, LANES)).reshape(scales, -1)
-    rest_w = jnp.broadcast_to(mine.T[:, :, None], (scales, slots, rest)).reshape(scales, -1)
-    rest_w = jnp.pad(rest_w, ((0, 0), (0, LANES - rest * slots)))
-    lane_wts = jnp.concatenate([main_w, rest_w], axis=1)
-
     gx = jnp.asarray(x_matrices(nt, rows, rows_pad))
     by = jnp.asarray(y_matrices(cols, slots, rest))
     picks = [jnp.asarray(a) for a in selectors(levels, nt, slots)]
@@ -419,13 +437,14 @@
     whole_wind = pltpu.VMEM((comps, nt, planes, rows_pad, LANES), f32)
     square = pltpu.VMEM((levels * SUB, levels * SUB), f32)
     dma = pltpu.SemaphoreType.DMA
-    return pl.pallas_call(
+    share = levels // nm // slots
+    wind_packed, back_packed = pl.pallas_call(
         functools.partial(kernel, dims),
         out_shape=(
-            jax.ShapeDtypeStruct((comps, levels // nm, rows, cols), f32),
-            jax.ShapeDtypeStruct(control.shape, f32),
+            jax.ShapeDtypeStruct((comps, share, planes, rows_pad, LANES), f32),
+            jax.ShapeDtypeStruct((members, nt, planes, rows_pad, LANES), f32),
         ),
-        in_specs=[vmem, anyspace, vmem, vmem, anyspace, anyspace, vmem, vmem, vmem],
+        in_specs=[vmem, anyspace, vmem, vmem, vmem, anyspace, anyspace, vmem, vmem, vmem],
         out_specs=(vmem, vmem),
         scratch_shapes=[
             pltpu.VMEM(ens_perts.shape[1:], f32),
@@ -442,6 +461,7 @@
             pltpu.VMEM((3 * all_x, planes * LANES), bf16),
             pltpu.VMEM((scales, planes, all_x, LANES), bf16),
             pltpu.VMEM((scales, planes, all_x, LANES), bf16),
+            pltpu.VMEM((scales, planes * LANES), f32),
             square, square, square, square,
             dma((3,)),
             dma((members,)), dma((members,)),
@@ -456,7 +476,29 @@
             collective_id=0, has_side_effects=True, vmem_limit_bytes=58 * 2 ** 20),
         cost_estimate=pl.CostEstimate(
             flops=12 * 10 ** 9, bytes_accessed=30 * 10 ** 6, transcendentals=0),
-    )(control, ens_perts, vert_corr, lane_wts, gx, by, *picks)
+    )(control, ens_perts, vert_corr, slab_wts, level_slab.reshape(1, levels), gx, by, *picks)
+
+    halves = 2
+    by_half = lambda n: (n // halves, n % halves, 0, 0)
+    all_wind = pl.BlockSpec(wind_packed.shape, lambda n: (0, 0, 0, 0, 0))
+    field_block = pl.BlockSpec((1, levels // halves, rows, cols), by_half)
+    wind_shape = (comps, levels // nm, rows, cols)
+    gradient, wind_share = pl.pallas_call(
+        functools.partial(unpack_kernel, rest),
+        grid=(members * halves,),
+        out_shape=(
+            jax.ShapeDtypeStruct(control.shape, f32), jax.ShapeDtypeStruct(wind_shape, f32)),
+        in_specs=[
+            field_block,
+            pl.BlockSpec((1, nt // halves, planes, rows_pad, LANES), lambda n: by_half(n) + (0,)),
+            all_wind,
+        ],
+        out_specs=(field_block, pl.BlockSpec(wind_shape, lambda n: (0, 0, 0, 0))),
+        compiler_params=pltpu.CompilerParams(vmem_limit_bytes=58 * 2 ** 20),
+        cost_estimate=pl.CostEstimate(
+            flops=2 * 10 ** 6, bytes_accessed=8 * 10 ** 6, transcendentals=0),
+    )(control, back_packed, wind_packed)
+    return wind_share, gradient
 
 
 def solution(mesh):

time: 167 us -> 161 us (0.964); the launches traced: 167 us -> 159 us
  local copies, waits for them, and re-layouts: 6.47 us -> 1.35 us
    pallas_call x1, Pallas kernels: 158 us -> 152 us  [shards(): pl.pallas_call(functools.partial(kernel, dims), out_shape=(jax.ShapeDtype...]
    pallas_call x0 -> x1, Pallas kernels: none -> 4.93 us  [shards(): pl.pallas_call(functools.partial(unpack_kernel, rest), grid=(members * ha...]
    unnamed x4 -> x1, local copies, waits for them, and re-layouts: 5.48 us -> 1.35 us
where the time goes in v1:
time: 161 us; the launch traced here: 159 us
  Pallas kernels  157 us (98%)
    pallas_call x1, Pallas kernels, shards(): pl.pallas_call(functools.partial(kernel, dims), out_shape=(jax.ShapeDtype...  152 us
    pallas_call x1, Pallas kernels, shards(): pl.pallas_call(functools.partial(unpack_kernel, rest), grid=(members * ha...  4.93 us

profile of v1, /device:TPU:13, one launch (start us, length us, event | category | flops | bytes accessed | tf_op | source)
XLA Modules:
  0.0 158.9 jit_solution(8612142419608712539)
XLA Ops:
  0.6 1.3 copy.12.slab_ref
  2.0 152.0 %shard_map.113 = (f32[2,2,5,40,128]{4,3,2,1,0:T(8,128)}, f32[2,8,5,40,128]{4,3,2,1,0:T(8,128)}) custom-call(f32[2,32,40,160]{3,2,1,0:T(8,128)} %control_ref.3, f32[2,2,32,40,160]{4,3,2,1,0:T(8,128)} %pert_hbm.1, f32[32,32]{1,0:T(8,128)} %vert_ref.1, f32[8,4]{1,0:T(8,128)} %copy.12.slab_ref, s32[1,32]{1,0:T(1,128)} %bitcast.1, ...), custom_call_target="tpu_custom_call" | custom-call | flops 12000000000 | bytes 30000000 | tf_op jit(solution)/shard_map/pallas_call | solution.py:441
  154.0 4.9 %shard_map.114 = (f32[2,32,40,160]{3,2,1,0:T(8,128)}, f32[2,8,40,160]{3,2,1,0:T(8,128)}) custom-call(f32[2,32,40,160]{3,2,1,0:T(8,128)} %control_ref.3, f32[2,8,5,40,128]{4,3,2,1,0:T(8,128)} %get-tuple-element.6.back_ref, f32[2,2,5,40,128]{4,3,2,1,0:T(8,128)} %get-tuple-element.7.wind_packed), custom_call_target="tpu_custom_call" | custom-call | flops 2000000 | bytes 8000000 | tf_op jit(solution)/shard_map/pallas_call | solution.py:486

commit v2 on v1

--- a/solution.py
+++ b/solution.py
@@ -76,11 +76,11 @@
 
 def kernel(
     dims,
-    control_ref, pert_hbm, vert_ref, slab_ref, level_ref, gx_hbm, by_hbm, main_sel, outer_sel, inner_sel,
-    wind_ref, back_ref,
-    pert_raw, gx, by, send_a, f_a, y_a, s_a, pert, wp, cr, ws, xr, wf, send_b, f_b, y_b,
+    control_hbm, pert_hbm, vert_ref, slab_ref, level_ref, gx_hbm, by_hbm, main_sel, outer_sel, inner_sel,
+    wind_hbm, back_hbm,
+    control_ref, pert_raw, gx, by, send_a, f_a, y_a, s_a, pert, wp, cr, ws, xr, wf, send_b, f_b, y_b,
     fs, xh, xl, wl_ref, mix_main, mix_rest, back_main, back_rest,
-    load_sem, a1s, a1r, a2s, a2r, a3s, a3r, a4s, a4r, c1s, c1r, xs, xrs, c2s, c2r,
+    load_sem, field_sem, out_sem, a1s, a1r, a2s, a2r, a3s, a3r, a4s, a4r, c1s, c1r, xs, xrs, c2s, c2r,
 ):
     nt, nm, members, comps, levels, rows, rows_pad, cols, slots, rest, scale, order = dims
     planes = slots + 1
@@ -100,7 +100,11 @@
         pltpu.make_async_copy(gx_hbm, gx, load_sem.at[1]),
         pltpu.make_async_copy(by_hbm, by, load_sem.at[2]),
     ]
-    for load in loads:
+    fields_in = [
+        pltpu.make_async_copy(control_hbm.at[m], control_ref.at[m], field_sem.at[m])
+        for m in range(members)
+    ]
+    for load in fields_in + loads:
         load.start()
 
     def packed(block):
@@ -127,6 +131,8 @@
         pl.semaphore_signal(barrier, inc=1, device_id={"mem": other}, device_id_type=MESH)
 
     def pack_control(m):
+        fields_in[m].wait()
+
         def body(t, carry):
             pack_to(control_ref[m, pl.ds(slots * t, slots)], send_a.at[m, t])
             return carry
@@ -161,15 +167,14 @@
         exchange(send_a, f_a, m, 0, rows_pad, a1s.at[m], a1r.at[m])
 
     vert = vert_ref[...]
-    slabs = slab_ref.shape[0]
-    column = lambda a, b: lax.dot_general(
-        a, b, (((0,), (0,)), ((), ())), precision=highest, preferred_element_type=f32)
+    slabs = slab_ref.shape[1]
+    exact = functools.partial(jnp.dot, precision=highest, preferred_element_type=f32)
     choose = (
         lax.broadcasted_iota(jnp.int32, (slabs, levels), 0) == level_ref[...]).astype(f32)
     lane = lax.broadcasted_iota(jnp.int32, (levels, planes * LANES), 1)
     lane_slot = jnp.where(lane < slots * LANES, lane // LANES, (lane - slots * LANES) // rest)
     own = (lax.broadcasted_iota(jnp.int32, lane.shape, 0) == me * slots + lane_slot).astype(f32)
-    wl_ref[...] = column(column(choose, slab_ref[...]), own)
+    wl_ref[...] = exact(exact(slab_ref[...], choose), own)
     same_row = lambda a, b: (
         lax.rem(lax.broadcasted_iota(jnp.int32, (a, b), 0), SUB)
         == lax.rem(lax.broadcasted_iota(jnp.int32, (a, b), 1), SUB)
@@ -336,13 +341,14 @@
             if m == 0 or c < early:
                 send_adjoint(m, c)
 
+    ahead = min(3, chunks)
     give_back = lambda m, c: exchange(y_a, s_a, m, c * SUB, SUB, a2s.at[m, c], a2r.at[m, c])
     for m in range(members):
         arrived(f_a, m, 0, rows_pad, a1r.at[m])
         smooth(f_a, m, y_a)
-        for c in range(early):
+        for c in range(ahead):
             give_back(m, c)
-    for c in range(early, chunks):
+    for c in range(ahead, chunks):
         for m in range(members):
             give_back(m, c)
 
@@ -360,8 +366,10 @@
         for c in range(early, chunks):
             send_adjoint(m, c)
 
-    share = wind_ref.shape[1]
-    wind_ref[...] = wf[:, pl.ds(mem * share, share)]
+    share = wind_hbm.shape[1]
+    results = [pltpu.make_async_copy(
+        wf.at[:, pl.ds(mem * share, share)], wind_hbm, out_sem.at[members])]
+    results[0].start()
 
     for m in range(members):
         for c in range(chunks):
@@ -371,8 +379,11 @@
 
     for m in range(members):
         arrived(s_b, m, 0, rows_pad, a4r.at[m])
-        back_ref[m] = s_b[m]
-
+        results.append(pltpu.make_async_copy(s_b.at[m], back_hbm.at[m], out_sem.at[m]))
+        results[-1].start()
+
+    for result in results:
+        result.wait()
     for m in range(members):
         sent(send_a, m, 0, rows_pad, a1s.at[m])
         sent(y_b, m, 0, rows_pad, a4s.at[m])
@@ -444,9 +455,10 @@
             jax.ShapeDtypeStruct((comps, share, planes, rows_pad, LANES), f32),
             jax.ShapeDtypeStruct((members, nt, planes, rows_pad, LANES), f32),
         ),
-        in_specs=[vmem, anyspace, vmem, vmem, vmem, anyspace, anyspace, vmem, vmem, vmem],
-        out_specs=(vmem, vmem),
+        in_specs=[anyspace, anyspace, vmem, vmem, vmem, anyspace, anyspace, vmem, vmem, vmem],
+        out_specs=(anyspace, anyspace),
         scratch_shapes=[
+            pltpu.VMEM(control.shape, f32),
             pltpu.VMEM(ens_perts.shape[1:], f32),
             pltpu.VMEM(gx.shape, bf16),
             pltpu.VMEM(by.shape, bf16),
@@ -463,7 +475,7 @@
             pltpu.VMEM((scales, planes, all_x, LANES), bf16),
             pltpu.VMEM((scales, planes * LANES), f32),
             square, square, square, square,
-            dma((3,)),
+            dma((3,)), dma((members,)), dma((members + 1,)),
             dma((members,)), dma((members,)),
             dma((members, chunks)), dma((members, chunks)),
             dma((members, chunks)), dma((members, chunks)),
@@ -476,7 +488,7 @@
             collective_id=0, has_side_effects=True, vmem_limit_bytes=58 * 2 ** 20),
         cost_estimate=pl.CostEstimate(
             flops=12 * 10 ** 9, bytes_accessed=30 * 10 ** 6, transcendentals=0),
-    )(control, ens_perts, vert_corr, slab_wts, level_slab.reshape(1, levels), gx, by, *picks)
+    )(control, ens_perts, vert_corr, slab_wts.T, level_slab.reshape(1, levels), gx, by, *picks)
 
     halves = 2
     by_half = lambda n: (n // halves, n % halves, 0, 0)

time: 161 us -> 156 us (0.969)
  Pallas kernels: 157 us -> 153 us
    pallas_call x1, Pallas kernels: 152 us -> 148 us  [shards(): pl.pallas_call(functools.partial(kernel, dims), out_shape=(jax.ShapeDtype...]
where the time goes in v2:
time: 156 us; the launch traced here: 154 us
  Pallas kernels  153 us (98%)
    pallas_call x1, Pallas kernels, shards(): pl.pallas_call(functools.partial(kernel, dims), out_shape=(jax.ShapeDtype...  148 us
    pallas_call x1, Pallas kernels, shards(): pl.pallas_call(functools.partial(unpack_kernel, rest), grid=(members * ha...  4.93 us

profile of v2, /device:TPU:13, one launch (start us, length us, event | category | flops | bytes accessed | tf_op | source)
XLA Modules:
  0.0 154.0 jit_solution(4745920175772119324)
XLA Ops:
  0.6 148.4 %shard_map.113 = (f32[2,2,5,40,128]{4,3,2,1,0:T(8,128)}, f32[2,8,5,40,128]{4,3,2,1,0:T(8,128)}) custom-call(f32[2,32,40,160]{3,2,1,0:T(8,128)} %control_ref.1, f32[2,2,32,40,160]{4,3,2,1,0:T(8,128)} %pert_hbm.1, f32[32,32]{1,0:T(8,128)} %vert_ref.1, f32[4,8]{1,0:T(4,128)} %bitcast.2, s32[1,32]{1,0:T(1,128)} %bitcast.3, ...), custom_call_target="tpu_custom_call" | custom-call | flops 12000000000 | bytes 30000000 | tf_op jit(solution)/shard_map/pallas_call | solution.py:452
  149.0 4.9 %shard_map.114 = (f32[2,32,40,160]{3,2,1,0:T(8,128)}, f32[2,8,40,160]{3,2,1,0:T(8,128)}) custom-call(f32[2,32,40,160]{3,2,1,0:T(8,128)} %control_ref.1, f32[2,8,5,40,128]{4,3,2,1,0:T(8,128)} %get-tuple-element.6.back_ref, f32[2,2,5,40,128]{4,3,2,1,0:T(8,128)} %get-tuple-element.7.wind_packed), custom_call_target="tpu_custom_call" | custom-call | flops 2000000 | bytes 8000000 | tf_op jit(solution)/shard_map/pallas_call | solution.py:498
